TPU v7x, 128 devices: a whole 4x4x4 slice. The times are simulated.
128 devices in a mesh: group: 16 (over x, z), inner: 8 (over y, core).
Axes of the slice: x: 4, y: 4, z: 4, core: 2. Of those that a mesh axis runs over, the one named last changes fastest.
Arguments:
- densities: float32 [1024, 64, 64], P('group'), may hold values from -1 to 2, as said below
- ref_charge: float32 [1024, 16], P('group'), may hold values from 2.1 to 3.1
- site_pos: float32 [3, 16384], P(None, 'group'), may hold values from 0 to 48
- dimer_pairs: int32 [256, 2], replicated, may hold values from 0 to 1023, as said below
- probe_pos: float32 [3, 2048], P(None, ('group', 'inner')), may hold values from 0 to 48
- core_ham: float32 [256, 128, 128], P(('group', 'inner')), may hold values from -4 to 4
- probe_ints: bfloat16 [256, 8, 128, 128], P(('group', 'inner')), may hold values from -0.375 to 0.375
- ri_ints: bfloat16 [256, 256, 128, 128], P(('group', 'inner')), may hold values from -0.1875 to 0.1875
Outputs:
- frag_weight: float32 [1024, 64, 64], P('group', 'inner')
- dimer_energy: float32 [256], P(('group', 'inner'))
Inputs may be any that keep to these rules, and one draw needn't show every extreme that they name: `densities`: symmetric in the last two dimensions. `dimer_pairs`: the two fragments of a dimer differ; within the 16 rows of one group no fragment appears twice, and at most 4 of them lie in the block of 64 fragments owned by one group. In every draw one owning group gives exactly 4 fragments to every group.
All inputs are finite; a program needn't handle non-finite values.
Results may differ from a plain program's by a relative error of at most 0.0035.
Values sent between devices are 32-bit elements; how exact they have to be, the bound alone decides.
No kernel may reach another device: no remote copies, remote signals or barrier semaphores. Data moves between devices by JAX's collectives and lax.ppermute only.
A program may use at most 128 MiB of HBM per device.

v0:
```python
import jax
import jax.numpy as jnp
from jax import lax
from jax.experimental import pallas as pl
from jax.experimental.pallas import tpu as pltpu
from jax.sharding import PartitionSpec as P

NB = 64
NB2 = 128
NAUX = 256
ATOMS = 16
NPROBE = 8
ITERS = 3
FRAG_GRP = 64
DIM_GRP = 16
CAP = 4
N_GROUP = 16
N_Y = 4
SITE_ROWS = 8
HALF = SITE_ROWS // 2
ROWS = NB + 4 * HALF
STRIDE = 8

STEP = 64
PART = 4
CHUNKS = 4

damping = 0.1
highest = lax.Precision.HIGHEST
VMEM = pl.BlockSpec(memory_space=pltpu.VMEM)
SMEM = pl.BlockSpec(memory_space=pltpu.SMEM)
ANY = pl.BlockSpec(memory_space=pl.ANY)


def dot32(a, b):
    return jnp.dot(a, b, precision=highest, preferred_element_type=jnp.float32)


def iota(shape, dim):
    return lax.broadcasted_iota(jnp.int32, shape, dim)


def endpoint(pairs, group, e):
    return pairs[e % 2, group * DIM_GRP + e // 2]


def owner_of(frag):
    return lax.shift_right_logical(frag, 6)


def pack_kernel(pos, pairs, dens_hbm, ref_charge, site_pos, send, table, dens, sem):
    group, core = pos[0], pos[2]
    load = pltpu.make_async_copy(dens_hbm, dens, sem)
    load.start()

    def list_group(g, carry):
        count = jnp.int32(0)
        for e in range(2 * DIM_GRP):
            frag = endpoint(pairs, g, e)
            table[g * STRIDE + count] = lax.bitwise_and(frag, FRAG_GRP - 1)
            count = count + (owner_of(frag) == group).astype(jnp.int32)
        table[g * STRIDE + STRIDE - 1] = count
        return carry

    lax.fori_loop(0, N_GROUP, list_group, 0)
    load.wait()

    eye = iota((NB, NB), 0) == iota((NB, NB), 1)
    diagonal = jnp.sum(jnp.where(eye[None], dens[...], 0.0), axis=1)
    spread = (iota((NB, 128), 0) // (NB // ATOMS) == iota((NB, 128), 1) % ATOMS).astype(jnp.float32)
    repeat = (iota((ATOMS, 128), 0) == iota((ATOMS, 128), 1) % ATOMS).astype(jnp.float32)
    charge = dot32(ref_charge[...], repeat) - dot32(diagonal, spread)
    mine = iota((FRAG_GRP, 128), 0) % (128 // ATOMS) == iota((FRAG_GRP, 128), 1) // ATOMS
    charge = jnp.sum(jnp.where(mine, charge, 0.0).reshape(SITE_ROWS, 128 // ATOMS, 128), axis=1)

    def half_of(rows):
        return jnp.where(core == 0, rows[:HALF], rows[HALF:])

    sites = jnp.concatenate([half_of(site_pos[c]) for c in range(3)] + [half_of(charge)], axis=0)

    def fill(g, carry):
        count = table[g * STRIDE + STRIDE - 1]
        pair = []
        for s in range(2):
            slot = 2 * core + s
            pair.append(dens[jnp.where(slot < count, table[g * STRIDE + slot], 0)])
        send[g, :NB] = jnp.concatenate(pair, axis=1)
        send[g, NB:] = sites
        return carry

    lax.fori_loop(0, N_GROUP, fill, 0)


def scf_kernel(pos, pairs, probe_pos, mine, other, core_ham, probe_ints, ri_hbm,
               keep, give, energy, ri, start, fixed, dens, packed, fock, weighted, sems):
    group, chip, core = pos[0], pos[1], pos[2]
    steps = NAUX // STEP
    per_chunk = NAUX // CHUNKS

    def load(c):
        part = pl.ds(c * per_chunk, per_chunk)
        return pltpu.make_async_copy(ri_hbm.at[:, part], ri.at[:, part], sems.at[c])

    for c in range(CHUNKS):
        load(c).start()

    first_dimer = (2 * chip + core) * 2
    left = iota((NB, NB2), 1) < NB

    def fragment_rows(dimer, side):
        e = 2 * dimer + side
        owner = owner_of(pairs[side, group * DIM_GRP + dimer])
        rank = jnp.int32(0)
        for k in range(2 * DIM_GRP):
            hit = jnp.logical_and(owner_of(endpoint(pairs, group, k)) == owner, k < e)
            rank = rank + hit.astype(jnp.int32)
        rows = jnp.where(rank // 2 == core, mine[owner, :NB], other[owner, :NB])
        return jnp.where(rank % 2 == side, rows, pltpu.roll(rows, NB, 1))

    for d in range(2):
        start[d, :NB] = jnp.where(left, fragment_rows(first_dimer + d, 0), 0.0)
        start[d, NB:] = jnp.where(left, 0.0, fragment_rows(first_dimer + d, 1))
        dens[d] = start[d]

    def gathered(c):
        rows = slice(NB + HALF * c, NB + HALF * (c + 1))
        return jnp.concatenate([mine[:, rows], other[:, rows]], axis=1)

    xs, ys, zs, charge = (gathered(c) for c in range(4))
    shape = (N_GROUP, SITE_ROWS, 128)
    row = iota(shape, 1)
    row = jnp.where(row < HALF, row + HALF * core, row - HALF * core)
    site_frag = iota(shape, 0) * FRAG_GRP + row * (128 // ATOMS) + iota(shape, 2) // ATOMS
    for d in range(2):
        column = group * DIM_GRP + first_dimer + d
        keep_site = jnp.logical_and(site_frag != pairs[0, column], site_frag != pairs[1, column])
        kept = jnp.where(keep_site, charge, 0.0)
        total = core_ham[d]
        for k in range(NPROBE):
            at = d * NPROBE + k
            dx, dy, dz = xs - probe_pos[0, at], ys - probe_pos[1, at], zs - probe_pos[2, at]
            terms = kept * lax.rsqrt(dx * dx + dy * dy + dz * dz + 1.0)
            weight = jnp.sum(jnp.sum(terms, axis=0), axis=(0, 1), keepdims=True)
            total = total + weight * probe_ints[d, k].astype(jnp.float32)
        fixed[d] = total

    eye = iota((NB2, NB2), 0) == iota((NB2, NB2), 1)
    zero = jnp.zeros((NB2, NB2), jnp.bfloat16)

    def accumulate(step):
        both = jnp.concatenate([jnp.concatenate([packed[0], zero], axis=1),
                                jnp.concatenate([zero, packed[1]], axis=1)], axis=0)
        sums = [fock[0], fock[1]]
        for g in range(STEP // PART):
            at = pl.ds(step * STEP + g * PART, PART)
            parts = [ri[d, at] for d in range(2)]
            wide = jnp.concatenate([p.reshape(PART * NB2, NB2) for p in parts], axis=1)
            half = jnp.dot(wide, both, preferred_element_type=jnp.float32)
            rows = []
            for d in range(2):
                blocks = []
                for i in range(PART):
                    block = half[i * NB2:(i + 1) * NB2, d * NB2:(d + 1) * NB2]
                    fit = (parts[d][i] * packed[d]).astype(jnp.float32).reshape(-1, 8, NB2)
                    fit = jnp.sum(jnp.sum(fit, axis=0), axis=(0, 1), keepdims=True)
                    fit = -2.0 * fit.astype(jnp.bfloat16).astype(jnp.float32)
                    blocks.append(jnp.where(eye, block + fit, block).astype(jnp.bfloat16))
                rows.append(jnp.concatenate(blocks, axis=1))
            out = jnp.dot(jnp.concatenate(rows, axis=0), wide, preferred_element_type=jnp.float32)
            sums[0] = sums[0] + out[:NB2, :NB2]
            sums[1] = sums[1] + out[NB2:, NB2:]
        fock[0] = sums[0]
        fock[1] = sums[1]

    def sweep(t, carry):
        packed[...] = dens[...].astype(jnp.bfloat16)
        fock[...] = jnp.zeros_like(fock)

        def body(step, inner_carry):
            @pl.when(t == 0)
            def _():
                load(step).wait()

            accumulate(step)
            return inner_carry

        lax.fori_loop(0, steps, body, 0)
        for d in range(2):
            matrix = fixed[d] - 0.5 * fock[d]
            fock[d] = matrix
            dens[d] = start[d] - damping * dot32(dot32(start[d], matrix), start[d])
        return carry

    lax.fori_loop(0, ITERS, sweep, 0)

    for d in range(2):
        matrix, density = fock[d], dens[d]
        energy[d] = (0.5 / NB2) * jnp.sum(density * (core_ham[d] + matrix))
        block = dot32(dot32(density, matrix), density)
        weighted[d] = jnp.where(left, block[:NB], block[NB:])
    for k in range(N_Y):
        for d in range(2):
            rows = 2 * lax.rem(chip + k, N_Y)
            keep[k, d] = weighted[d, pl.ds(pl.multiple_of((rows + core) * 8, 8), 8)]
            give[k, d] = weighted[d, pl.ds(pl.multiple_of((rows + 1 - core) * 8, 8), 8)]


def route_kernel(pos, pairs, own0, own1, got1, got2, got3, out, count, owners, ranks):
    group, chip, core = pos[0], pos[1], pos[2]
    for o in range(N_GROUP):
        count[o] = 0
    for e in range(2 * DIM_GRP):
        owner = owner_of(endpoint(pairs, group, e))
        rank = count[owner]
        owners[e] = owner
        ranks[e] = rank
        count[owner] = rank + 1
    out[...] = jnp.zeros_like(out)
    lane_half = iota((8, 128), 1) // NB
    for k in range(N_Y):
        for src in range(2):
            for d in range(2):
                if k == 0:
                    block = (own0, own1)[src][d]
                else:
                    block = (got1, got2, got3)[k - 1][src, d]
                turned = pltpu.roll(block, NB, 1)
                from_core = core if src == 0 else 1 - core
                dimer = (2 * lax.rem(chip - k + N_Y, N_Y) + from_core) * 2 + d
                for side in range(2):
                    owner, rank = owners[2 * dimer + side], ranks[2 * dimer + side]
                    half = lax.rem(rank, 2)
                    value = jnp.where(half == side, block, turned)
                    here = (owner, lax.div(rank, 2))
                    out[here] = jnp.where(lane_half == half, value, out[here])


def home_kernel(table, got, out):
    out[...] = jnp.zeros_like(out)

    def add(g, carry):
        count = table[g * STRIDE + STRIDE - 1]
        for s in range(CAP):
            at = jnp.where(s < count, table[g * STRIDE + s], 0)
            block = got[g, s // 2]
            value = block[:, :NB] if s % 2 == 0 else pltpu.roll(block, NB, 1)[:, :NB]
            out[at] = out[at] + jnp.where(s < count, value, 0.0)
        return carry

    lax.fori_loop(0, N_GROUP, add, 0)


def params(mib):
    return pltpu.CompilerParams(vmem_limit_bytes=mib * 1024 * 1024)


def per_device(densities, ref_charge, site_pos, dimer_pairs, probe_pos, core_ham, probe_ints, ri_ints):
    f32, i32 = jnp.float32, jnp.int32
    inner = lax.axis_index("inner")
    pos = jnp.stack([lax.axis_index("group"), inner // 2, inner % 2]).astype(i32)
    pairs = dimer_pairs.T
    n_inner = 2 * N_Y
    swap = [(i, i ^ 1) for i in range(n_inner)]

    with jax.named_scope("pack"):
        send, table = pl.pallas_call(
            pack_kernel,
            out_shape=(jax.ShapeDtypeStruct((N_GROUP, ROWS, 128), f32),
                       jax.ShapeDtypeStruct((N_GROUP * STRIDE,), i32)),
            in_specs=[SMEM, SMEM, ANY, VMEM, VMEM],
            out_specs=(VMEM, SMEM),
            scratch_shapes=[pltpu.VMEM((FRAG_GRP, NB, NB), f32), pltpu.SemaphoreType.DMA],
            compiler_params=params(16),
            name="pack",
        )(pos, pairs, densities, ref_charge, site_pos.reshape(3, SITE_ROWS, 128))
    mine = lax.all_to_all(send, "group", split_axis=0, concat_axis=0, tiled=True)
    other = lax.ppermute(mine, "inner", swap)

    with jax.named_scope("scf"):
        piece = jax.ShapeDtypeStruct((N_Y, 2, 8, 128), f32)
        square = pltpu.VMEM((2, NB2, NB2), f32)
        keep, give, energy = pl.pallas_call(
            scf_kernel,
            out_shape=(piece, piece, jax.ShapeDtypeStruct((2,), f32)),
            in_specs=[SMEM, SMEM, SMEM, VMEM, VMEM, VMEM, VMEM, ANY],
            out_specs=(VMEM, VMEM, SMEM),
            scratch_shapes=[
                pltpu.VMEM((2, NAUX, NB2, NB2), jnp.bfloat16),
                square, square, square,
                pltpu.VMEM((2, NB2, NB2), jnp.bfloat16),
                square,
                pltpu.VMEM((2, NB, NB2), f32),
                pltpu.SemaphoreType.DMA((CHUNKS,)),
            ],
            compiler_params=params(40),
            name="scf",
        )(pos, pairs, probe_pos, mine, other, core_ham, probe_ints, ri_ints)
    partner = lax.ppermute(give, "inner", swap)
    got = []
    for k in range(1, N_Y):
        step = [(i, (i + 2 * k) % n_inner) for i in range(n_inner)]
        got.append(lax.ppermute(jnp.stack([keep[k], partner[k]]), "inner", step))

    with jax.named_scope("route"):
        slots = pl.pallas_call(
            route_kernel,
            out_shape=jax.ShapeDtypeStruct((N_GROUP, CAP // 2, 8, 128), f32),
            in_specs=[SMEM, SMEM] + [VMEM] * 5,
            out_specs=VMEM,
            scratch_shapes=[pltpu.SMEM((N_GROUP,), i32), pltpu.SMEM((2 * DIM_GRP,), i32),
                            pltpu.SMEM((2 * DIM_GRP,), i32)],
            name="route",
        )(pos, pairs, keep[0], partner[0], *got)
    homed = lax.all_to_all(slots, "group", split_axis=0, concat_axis=0, tiled=True)

    with jax.named_scope("home"):
        frag_weight = pl.pallas_call(
            home_kernel,
            out_shape=jax.ShapeDtypeStruct((FRAG_GRP, 8, NB), f32),
            in_specs=[SMEM, VMEM],
            out_specs=VMEM,
            name="home",
        )(table, homed)
    return (frag_weight, energy)


def solution(mesh):
    in_specs = (
        P("group", None, None),
        P("group", None),
        P(None, "group"),
        P(),
        P(None, ("group", "inner")),
        P(("group", "inner"), None, None),
        P(("group", "inner"), None, None, None),
        P(("group", "inner"), None, None, None),
    )
    out_specs = (P("group", "inner", None), P(("group", "inner")))
    return jax.shard_map(
        per_device, mesh=mesh, in_specs=in_specs, out_specs=out_specs, check_vma=False
    )
```

profile of v0, /device:TPU:0, one launch (start us, length us, event | category | flops | bytes accessed | tf_op | source)
XLA Modules:
  0.0 103.9 jit_solution(17238210100828116260)
XLA Ops:
  0.6 0.7 copy.13
  1.4 0.8 copy.10.ref_charge
  2.1 0.1 pad_add_fusion.pos
  2.2 0.0 copy-start.5
  2.2 0.0 copy-start
  2.2 1.6 %copy-done = f32[64,64,64]{2,1,0:T(8,128)S(1)} copy-done((f32[64,64,64]{2,1,0:T(8,128)S(1)}, f32[64,64,64]{2,1,0:T(8,128)}, u32[]{:S(2)}) %copy-start) | copy-done | bytes 1048600
  3.8 0.0 copy-start.3
  3.8 0.7 copy-done.3
  4.5 4.8 %pack.1 = (f32[16,80,128]{2,1,0:T(8,128)S(1)}, s32[128]{0:T(128)S(1)}) custom-call(s32[3]{0:T(128)S(1)} %pad_add_fusion.pos, s32[2,256]{1,0:T(2,128)S(1)} %bitcast.14, f32[64,64,64]{2,1,0:T(8,128)S(1)} %copy-done, f32[64,16]{1,0:T(8,128)S(1)} %copy.10.ref_charge, f32[3,8,128]{2,1,0:T(8,128)S(1)} %bitcast.12), custom_call_target="tpu_custom_call" | custom-call | tf_op jit(solution)/shard_map/pack/pack/pallas_call | solution.py:266
  9.3 0.0 copy-start.7
  9.3 20.5 %all_to_all.10.mine = f32[16,80,128]{2,1,0:T(8,128)S(1)} all-to-all(f32[16,80,128]{2,1,0:T(8,128)S(1)} %get-tuple-element.8), channel_id=1, replica_groups=mesh['group'=16,'inner'=8] {'group'}, dimensions={0} | all-to-all | bytes 1310720 | tf_op jit(solution)/shard_map/all_to_all | solution.py:276
  29.8 0.0 collective-permute-start
  29.8 0.0 copy-done.7
  29.8 2.1 %collective-permute-done.other = f32[16,80,128]{2,1,0:T(8,128)S(1)} collective-permute-done((f32[16,80,128]{2,1,0:T(8,128)S(1)}, f32[16,80,128]{2,1,0:T(8,128)S(1)}, u32[]{:S(2)}, u32[]{:S(2)}) %collective-permute-start) | collective-permute-done | bytes 655392 | tf_op jit(solution)/shard_map/ppermute | solution.py:277
  31.9 0.0 copy-start.1
  31.9 1.0 %copy-done.1 = bf16[2,8,128,128]{3,2,1,0:T(8,128)(2,1)S(1)} copy-done((bf16[2,8,128,128]{3,2,1,0:T(8,128)(2,1)S(1)}, bf16[2,8,128,128]{3,2,1,0:T(8,128)(2,1)}, u32[]{:S(2)}) %copy-start.1) | copy-done | bytes 524312
  33.0 0.0 copy-start.2
  33.0 0.9 copy-done.2
  33.9 0.0 copy-start.4
  33.9 0.7 copy-done.4
  34.6 0.0 copy-start.6
  34.6 0.7 copy-done.6
  35.2 41.3 %scf.1 = (f32[4,2,8,128]{3,2,1,0:T(8,128)S(1)}, f32[4,2,8,128]{3,2,1,0:T(8,128)S(1)}, f32[2]{0:T(128)}) custom-call(s32[3]{0:T(128)S(1)} %pad_add_fusion.pos, s32[2,256]{1,0:T(2,128)S(1)} %bitcast.15, f32[3,16]{1,0:T(4,128)S(1)} %copy-done.6, f32[16,80,128]{2,1,0:T(8,128)S(1)} %all_to_all.10.mine, f32[16,80,128]{2,1,0:T(8,128)S(1)} %collective-permute-done.other, ...), custom_call_target="tpu_custom_call" | custom-call | tf_op jit(solution)/shard_map/scf/scf/pallas_call | solution.py:282
  76.5 0.2 collective-permute-start.1
  76.7 0.6 fusion
  77.3 0.5 collective-permute-done.1
  77.8 0.6 fusion.1
  78.4 1.6 %collective-permute-start.2 = (f32[2,2,8,128]{3,2,1,0:T(8,128)S(1)}, f32[2,2,8,128]{3,2,1,0:T(8,128)S(1)}, u32[]{:S(2)}, u32[]{:S(2)}) collective-permute-start(f32[2,2,8,128]{3,2,1,0:T(8,128)S(1)} %pad_maximum_fusion), channel_id=1, source_target_pairs={{0,2},{1,3},{2,4},{3,5},{4,6},{5,7},{6,0},{7,1},{8,10},{9,11},{10,... | collective-permute-start | bytes 49160 | tf_op jit(solution)/shard_map/ppermute | solution.py:302
  80.0 2.9 %collective-permute-start.3 = (f32[2,2,8,128]{3,2,1,0:T(8,128)S(1)}, f32[2,2,8,128]{3,2,1,0:T(8,128)S(1)}, u32[]{:S(2)}, u32[]{:S(2)}) collective-permute-start(f32[2,2,8,128]{3,2,1,0:T(8,128)S(1)} %pad_maximum_fusion.1), channel_id=1, source_target_pairs={{0,4},{1,5},{2,6},{3,7},{4,0},{5,1},{6,2},{7,3},{8,12},{9,13},{10,... | collective-permute-start | bytes 49160 | tf_op jit(solution)/shard_map/ppermute | solution.py:302
  82.9 1.3 %collective-permute-start.4 = (f32[2,2,8,128]{3,2,1,0:T(8,128)S(1)}, f32[2,2,8,128]{3,2,1,0:T(8,128)S(1)}, u32[]{:S(2)}, u32[]{:S(2)}) collective-permute-start(f32[2,2,8,128]{3,2,1,0:T(8,128)S(1)} %pad_maximum_fusion.2), channel_id=1, source_target_pairs={{0,6},{1,7},{2,0},{3,1},{4,2},{5,3},{6,4},{7,5},{8,14},{9,15},{10,... | collective-permute-start | bytes 49160 | tf_op jit(solution)/shard_map/ppermute | solution.py:302
  84.2 0.0 collective-permute-done.2.got1
  84.2 0.0 copy-start.8
  84.2 1.0 collective-permute-done.3.got2
  85.2 0.0 copy-start.9
  85.2 1.4 %collective-permute-done.4.got3 = f32[2,2,8,128]{3,2,1,0:T(8,128)S(1)} collective-permute-done((f32[2,2,8,128]{3,2,1,0:T(8,128)S(1)}, f32[2,2,8,128]{3,2,1,0:T(8,128)S(1)}, u32[]{:S(2)}, u32[]{:S(2)}) %collective-permute-start.4) | collective-permute-done | bytes 16416 | tf_op jit(solution)/shard_map/ppermute | solution.py:302
  86.6 0.0 copy-start.10
  86.6 0.0 copy-done.5
  86.6 0.0 copy-done.8
  86.6 0.0 copy-done.9
  86.6 0.6 copy-done.10
  87.2 1.8 %route.1 = f32[16,2,8,128]{3,2,1,0:T(8,128)} custom-call(s32[3]{0:T(128)} %copy-done.5, s32[2,256]{1,0:T(2,128)} %bitcast.13, f32[2,8,128]{2,1,0:T(8,128)} %get-tuple-element.15.own0, f32[2,8,128]{2,1,0:T(8,128)} %get-tuple-element.19.own1, f32[2,2,8,128]{3,2,1,0:T(8,128)} %copy-done.8, f32[2,2,8,128]{3,2,1,0:T(8,128)} %copy-done.9, f32[2,2,8,128]{3,2,1,0:T(8,128)} %copy-done.10), custom_call_target="tpu_custom_call" | custom-call | tf_op jit(solution)/shard_map/route/route/pallas_call | solution.py:305
  89.0 12.0 %all_to_all.11.got = f32[16,2,8,128]{3,2,1,0:T(8,128)} all-to-all(f32[16,2,8,128]{3,2,1,0:T(8,128)} %route.1), channel_id=1, replica_groups=mesh['group'=16,'inner'=8] {'group'}, dimensions={0} | all-to-all | bytes 262144 | tf_op jit(solution)/shard_map/all_to_all | solution.py:314
  101.0 2.9 %home.1 = f32[64,8,64]{2,1,0:T(8,128)} custom-call(s32[128]{0:T(128)} %copy-done.7, f32[16,2,8,128]{3,2,1,0:T(8,128)} %all_to_all.11.got), custom_call_target="tpu_custom_call" | custom-call | tf_op jit(solution)/shard_map/home/home/pallas_call | solution.py:317
  (3 shorter events, 0.0 us)
Async XLA Ops:
  2.2 84.4 %copy-start.5 = (s32[3]{0:T(128)}, s32[3]{0:T(128)S(1)}, u32[]{:S(2)}) copy-start(s32[3]{0:T(128)S(1)} %pad_add_fusion.pos) | copy-start | bytes 40
  2.2 1.6 %copy-start = (f32[64,64,64]{2,1,0:T(8,128)S(1)}, f32[64,64,64]{2,1,0:T(8,128)}, u32[]{:S(2)}) copy-start(f32[64,64,64]{2,1,0:T(8,128)} %dens_hbm.1) | copy-start | bytes 3145732
  3.8 0.7 copy-start.3
  9.3 20.5 %copy-start.7 = (s32[128]{0:T(128)}, s32[128]{0:T(128)S(1)}, u32[]{:S(2)}) copy-start(s32[128]{0:T(128)S(1)} %get-tuple-element.7.table) | copy-start | bytes 1540
  29.8 2.1 %collective-permute-start = (f32[16,80,128]{2,1,0:T(8,128)S(1)}, f32[16,80,128]{2,1,0:T(8,128)S(1)}, u32[]{:S(2)}, u32[]{:S(2)}) collective-permute-start(f32[16,80,128]{2,1,0:T(8,128)S(1)} %all_to_all.10.mine), channel_id=1, source_target_pairs={{0,1},{1,0},{2,3},{3,2},{4,5},{5,4},{6,7},{7,6},{8,9},{9,8},{10,11... | collective-permute-start | bytes 1966088 | tf_op jit(solution)/shard_map/ppermute | solution.py:277
  31.9 1.0 %copy-start.1 = (bf16[2,8,128,128]{3,2,1,0:T(8,128)(2,1)S(1)}, bf16[2,8,128,128]{3,2,1,0:T(8,128)(2,1)}, u32[]{:S(2)}) copy-start(bf16[2,8,128,128]{3,2,1,0:T(8,128)(2,1)} %probe_ints.1) | copy-start | bytes 1572868
  33.0 0.9 copy-start.2
  33.9 0.7 copy-start.4
  34.6 0.7 copy-start.6
  76.5 1.3 %collective-permute-start.1 = (f32[4,2,8,128]{3,2,1,0:T(8,128)S(1)}, f32[4,2,8,128]{3,2,1,0:T(8,128)S(1)}, u32[]{:S(2)}, u32[]{:S(2)}) collective-permute-start(f32[4,2,8,128]{3,2,1,0:T(8,128)S(1)} %get-tuple-element.10), channel_id=1, source_target_pairs={{0,1},{1,0},{2,3},{3,2},{4,5},{5,4},{6,7},{7,6},{8,9},{9,8},{10,11... | collective-permute-start | bytes 98312 | tf_op jit(solution)/shard_map/ppermute | solution.py:298
  78.4 5.8 %collective-permute-start.2 = (f32[2,2,8,128]{3,2,1,0:T(8,128)S(1)}, f32[2,2,8,128]{3,2,1,0:T(8,128)S(1)}, u32[]{:S(2)}, u32[]{:S(2)}) collective-permute-start(f32[2,2,8,128]{3,2,1,0:T(8,128)S(1)} %pad_maximum_fusion), channel_id=1, source_target_pairs={{0,2},{1,3},{2,4},{3,5},{4,6},{5,7},{6,0},{7,1},{8,10},{9,11},{10,... | collective-permute-start | bytes 49160 | tf_op jit(solution)/shard_map/ppermute | solution.py:302
  80.0 5.2 %collective-permute-start.3 = (f32[2,2,8,128]{3,2,1,0:T(8,128)S(1)}, f32[2,2,8,128]{3,2,1,0:T(8,128)S(1)}, u32[]{:S(2)}, u32[]{:S(2)}) collective-permute-start(f32[2,2,8,128]{3,2,1,0:T(8,128)S(1)} %pad_maximum_fusion.1), channel_id=1, source_target_pairs={{0,4},{1,5},{2,6},{3,7},{4,0},{5,1},{6,2},{7,3},{8,12},{9,13},{10,... | collective-permute-start | bytes 49160 | tf_op jit(solution)/shard_map/ppermute | solution.py:302
  82.9 3.7 %collective-permute-start.4 = (f32[2,2,8,128]{3,2,1,0:T(8,128)S(1)}, f32[2,2,8,128]{3,2,1,0:T(8,128)S(1)}, u32[]{:S(2)}, u32[]{:S(2)}) collective-permute-start(f32[2,2,8,128]{3,2,1,0:T(8,128)S(1)} %pad_maximum_fusion.2), channel_id=1, source_target_pairs={{0,6},{1,7},{2,0},{3,1},{4,2},{5,3},{6,4},{7,5},{8,14},{9,15},{10,... | collective-permute-start | bytes 49160 | tf_op jit(solution)/shard_map/ppermute | solution.py:302
  84.2 2.4 %copy-start.8 = (f32[2,2,8,128]{3,2,1,0:T(8,128)}, f32[2,2,8,128]{3,2,1,0:T(8,128)S(1)}, u32[]{:S(2)}) copy-start(f32[2,2,8,128]{3,2,1,0:T(8,128)S(1)} %collective-permute-done.2.got1) | copy-start | bytes 49156
  85.2 1.4 %copy-start.9 = (f32[2,2,8,128]{3,2,1,0:T(8,128)}, f32[2,2,8,128]{3,2,1,0:T(8,128)S(1)}, u32[]{:S(2)}) copy-start(f32[2,2,8,128]{3,2,1,0:T(8,128)S(1)} %collective-permute-done.3.got2) | copy-start | bytes 49156
  86.6 0.6 copy-start.10
where the time goes:
time: 105 us; the launch traced here: 104 us
  Pallas kernels  50.8 us (48%)
  blocking collectives  32.5 us (31%)
  local copies, waits for them, and re-layouts  8.89 us (8%)
  starting transfers between devices  6.03 us (6%)
  waiting for transfers between devices  4.95 us (5%)
    pallas_call x1, Pallas kernels, per_device(): pl.pallas_call(scf_kernel, out_shape=(piece, piece, jax.ShapeDtypeStruct(...  41.3 us
    all_to_all x1, blocking collectives, per_device(): lax.all_to_all(send, 'group', split_axis=0, concat_axis=0, tiled=True)  20.5 us
    all_to_all x1, blocking collectives, per_device(): lax.all_to_all(slots, 'group', split_axis=0, concat_axis=0, tiled=True)  12 us
    unnamed x24, local copies, waits for them, and re-layouts  7.69 us
    ppermute x3, starting transfers between devices, per_device(): got.append(lax.ppermute(jnp.stack([keep[k], partner[k]]), 'inner', step))  5.82 us
    pallas_call x1, Pallas kernels, per_device(): pl.pallas_call(pack_kernel, out_shape=(jax.ShapeDtypeStruct((N_GROUP, ROW...  4.81 us
    pallas_call x1, Pallas kernels, per_device(): pl.pallas_call(home_kernel, out_shape=jax.ShapeDtypeStruct((FRAG_GRP, 8,...  2.92 us
    ppermute x3, waiting for transfers between devices, per_device(): got.append(lax.ppermute(jnp.stack([keep[k], partner[k]]), 'inner', step))  2.38 us
  transfers between devices with their start and end apart: 5, of which 4 were waited for; matrix products, arithmetic and copies ran while one was open for 1% of the time, Pallas kernels for 0%

commit v1 on v0

v1 whole, which is shorter than its diff:
```python
import jax
import jax.numpy as jnp
from jax import lax
from jax.experimental import pallas as pl
from jax.experimental.pallas import tpu as pltpu
from jax.sharding import PartitionSpec as P

NB = 64
NB2 = 128
NAUX = 256
ATOMS = 16
NPROBE = 8
ITERS = 3
FRAG_GRP = 64
DIM_GRP = 16
CAP = 4
N_GROUP = 16
N_INNER = 8
SITE_ROWS = 8
HALF = SITE_ROWS // 2
ROWS = NB + 4 * HALF

STEP = 128
PART = 4
CHUNKS = 4

damping = 0.1
highest = lax.Precision.HIGHEST
VMEM = pl.BlockSpec(memory_space=pltpu.VMEM)
SMEM = pl.BlockSpec(memory_space=pltpu.SMEM)
ANY = pl.BlockSpec(memory_space=pl.ANY)


def dot32(a, b):
    return jnp.dot(a, b, precision=highest, preferred_element_type=jnp.float32)


def iota(shape, dim):
    return lax.broadcasted_iota(jnp.int32, shape, dim)


def owner_of(frag):
    return lax.shift_right_logical(frag, 6)


def place():
    inner = lax.axis_index("inner")
    return lax.axis_index("group"), inner // 2, inner % 2


def pack_kernel(pairs, dens_hbm, ref_charge, site_pos, send, table, dens, found, sem, found_sem):
    group, _, core = place()
    load = pltpu.make_async_copy(dens_hbm, dens, sem)
    load.start()

    frags = pairs[...]
    mine = (owner_of(frags) == group).astype(jnp.float32)
    columns = pairs.shape[1]
    pad = jnp.zeros((14, columns), jnp.float32)
    hits = jnp.concatenate([mine, pad], axis=0).astype(jnp.bfloat16)
    rows, cols = iota((columns, columns), 0), iota((columns, columns), 1)
    together = rows // DIM_GRP == cols // DIM_GRP
    ahead = jnp.logical_and(together, rows < cols).astype(jnp.bfloat16)
    before = jnp.dot(hits, ahead, preferred_element_type=jnp.float32)
    in_all = jnp.dot(hits, together.astype(jnp.bfloat16), preferred_element_type=jnp.float32)
    rank = jnp.concatenate([before[0:1], before[1:2] + in_all[0:1]], axis=0)
    local = lax.bitwise_and(frags, FRAG_GRP - 1).astype(jnp.float32)
    entries = []
    for s in range(CAP):
        taken = jnp.where(rank == s, mine * local, 0.0)
        entries.append(taken[0:1] + taken[1:2])
    entries.append(mine[0:1] + mine[1:2])
    entries = jnp.concatenate(entries + [pad[:16 - len(entries)]], axis=0).astype(jnp.bfloat16)
    segment = (iota((columns, 128), 0) // DIM_GRP == iota((columns, 128), 1)).astype(jnp.bfloat16)
    entries = jnp.dot(entries, segment, preferred_element_type=jnp.float32)[:8].astype(jnp.int32)
    table[...] = entries
    tell = pltpu.make_async_copy(table, found, found_sem)
    tell.start()
    load.wait()

    blocks = dens[...].reshape(FRAG_GRP, NB // 8, 8, NB)
    lane = iota((FRAG_GRP, 8, NB), 2)
    diagonal = blocks[:, 0]
    for i in range(1, NB // 8):
        diagonal = jnp.where(lane // 8 == i, blocks[:, i], diagonal)
    diagonal = jnp.sum(jnp.where(lane % 8 == iota((FRAG_GRP, 8, NB), 1), diagonal, 0.0), axis=1)
    spread = (iota((NB, 128), 0) // (NB // ATOMS) == iota((NB, 128), 1) % ATOMS).astype(jnp.float32)
    repeat = (iota((ATOMS, 128), 0) == iota((ATOMS, 128), 1) % ATOMS).astype(jnp.float32)
    given = lax.dot_general(ref_charge[...], repeat, (((0,), (0,)), ((), ())),
                            precision=highest, preferred_element_type=jnp.float32)
    charge = given - dot32(diagonal, spread)
    here = iota((FRAG_GRP, 128), 0) % (128 // ATOMS) == iota((FRAG_GRP, 128), 1) // ATOMS
    charge = jnp.sum(jnp.where(here, charge, 0.0).reshape(SITE_ROWS, 128 // ATOMS, 128), axis=1)

    sites = []
    for c in range(3):
        for r in range(HALF):
            low = site_pos[c:c + 1, r * 128:(r + 1) * 128]
            high = site_pos[c:c + 1, (r + HALF) * 128:(r + HALF + 1) * 128]
            sites.append(jnp.where(core == 0, low, high))
    sites = jnp.concatenate(sites + [jnp.where(core == 0, charge[:HALF], charge[HALF:])], axis=0)

    tell.wait()
    for g in range(N_GROUP):
        pair = [dens[found[2 * core + s, g]] for s in range(2)]
        send[g, :NB] = jnp.concatenate(pair, axis=1)
        send[g, NB:] = sites


def scf_kernel(pairs, pairs_wide, probe_pos, mine, other, core_any, probes_any, ri_hbm,
               blocks, energy, ri, start, fixed, dens, packed, fock, weighted, frags, sites,
               core_ham, probe_ints, ri_sems, frag_sems, late_sems):
    group, chip, core = place()
    per_chunk = NAUX // CHUNKS

    def load(c, d):
        part = pl.ds(c * per_chunk, per_chunk)
        return pltpu.make_async_copy(ri_hbm.at[d, part], ri.at[d, part], ri_sems.at[c, d])

    def load_chunk(c):
        load(c, 0).start()
        load(c, 1).start()

    load_chunk(0)
    first_dimer = (2 * chip + core) * 2
    left = iota((NB, NB2), 1) < NB

    owners = owner_of(pairs_wide[...])
    column = iota(owners.shape, 1)
    in_group = column // DIM_GRP == group
    first_row = iota(owners.shape, 0) == 0

    def load_fragment(i):
        side = i % 2
        at = group * DIM_GRP + first_dimer + i // 2
        owner = owner_of(pairs[side, at])
        if side == 0:
            earlier = jnp.logical_and(first_row, column < at)
        else:
            earlier = jnp.logical_or(first_row, column < at)
        hit = jnp.logical_and(jnp.logical_and(owners == owner, in_group), earlier)
        rank = jnp.sum(hit.astype(jnp.int32))

        @pl.when(rank // 2 == core)
        def _():
            pltpu.make_async_copy(mine.at[owner, pl.ds(0, NB)], frags.at[i], frag_sems.at[i]).start()

        @pl.when(rank // 2 != core)
        def _():
            pltpu.make_async_copy(other.at[owner, pl.ds(0, NB)], frags.at[i], frag_sems.at[i]).start()

        return rank

    ranks = [load_fragment(i) for i in range(4)]
    late = [pltpu.make_async_copy(mine.at[:, pl.ds(NB, ROWS - NB)], sites.at[0], late_sems.at[0]),
            pltpu.make_async_copy(other.at[:, pl.ds(NB, ROWS - NB)], sites.at[1], late_sems.at[1]),
            pltpu.make_async_copy(core_any, core_ham, late_sems.at[2]),
            pltpu.make_async_copy(probes_any, probe_ints, late_sems.at[3])]

    for d in range(2):
        halves = []
        for side in range(2):
            i = 2 * d + side
            pltpu.make_async_copy(mine.at[0, pl.ds(0, NB)], frags.at[i], frag_sems.at[i]).wait()
            rows = frags[i]
            halves.append(jnp.where(ranks[i] % 2 == side, rows, pltpu.roll(rows, NB, 1)))
        start[d, :NB] = jnp.where(left, halves[0], 0.0)
        start[d, NB:] = jnp.where(left, 0.0, halves[1])
        dens[d] = start[d]

    def fill_fixed():
        def gathered(c):
            rows = slice(HALF * c, HALF * (c + 1))
            return jnp.concatenate([sites[0, :, rows], sites[1, :, rows]], axis=1)

        xs, ys, zs, charge = (gathered(c) for c in range(4))
        shape = (N_GROUP, SITE_ROWS, 128)
        row = iota(shape, 1)
        row = jnp.where(row < HALF, row + HALF * core, row - HALF * core)
        site_frag = iota(shape, 0) * FRAG_GRP + row * (128 // ATOMS) + iota(shape, 2) // ATOMS
        for d in range(2):
            at = group * DIM_GRP + first_dimer + d
            keep_site = jnp.logical_and(site_frag != pairs[0, at], site_frag != pairs[1, at])
            kept = jnp.where(keep_site, charge, 0.0)
            total = core_ham[d]
            for k in range(NPROBE):
                p = d * NPROBE + k
                dx, dy, dz = xs - probe_pos[0, p], ys - probe_pos[1, p], zs - probe_pos[2, p]
                terms = kept * lax.rsqrt(dx * dx + dy * dy + dz * dz + 1.0)
                weight = jnp.sum(jnp.sum(terms, axis=0), axis=(0, 1), keepdims=True)
                total = total + weight * probe_ints[d, k].astype(jnp.float32)
            fixed[d] = total

    eye = iota((NB2, NB2), 0) == iota((NB2, NB2), 1)
    zero = jnp.zeros((NB2, NB2), jnp.bfloat16)

    def accumulate(first, count):
        both = jnp.concatenate([jnp.concatenate([packed[0], zero], axis=1),
                                jnp.concatenate([zero, packed[1]], axis=1)], axis=0)
        sums = [fock[0], fock[1]]
        for g in range(count // PART):
            at = pl.ds(first + g * PART, PART)
            parts = [ri[d, at] for d in range(2)]
            wide = jnp.concatenate([p.reshape(PART * NB2, NB2) for p in parts], axis=1)
            half = jnp.dot(wide, both, preferred_element_type=jnp.float32)
            rows = []
            for d in range(2):
                squares = []
                for i in range(PART):
                    square = half[i * NB2:(i + 1) * NB2, d * NB2:(d + 1) * NB2]
                    fit = (parts[d][i] * packed[d]).astype(jnp.float32).reshape(-1, 8, NB2)
                    fit = jnp.sum(jnp.sum(fit, axis=0), axis=0, keepdims=True)
                    fit = jnp.sum(fit, axis=1, keepdims=True)
                    fit = -2.0 * fit.astype(jnp.bfloat16).astype(jnp.float32)
                    squares.append(jnp.where(eye, square + fit, square).astype(jnp.bfloat16))
                rows.append(jnp.concatenate(squares, axis=1))
            out = jnp.dot(jnp.concatenate(rows, axis=0), wide, preferred_element_type=jnp.float32)
            sums[0] = sums[0] + out[:NB2, :NB2]
            sums[1] = sums[1] + out[NB2:, NB2:]
        fock[0] = sums[0]
        fock[1] = sums[1]

    def begin():
        packed[...] = dens[...].astype(jnp.bfloat16)
        fock[...] = jnp.zeros_like(fock)

    def update():
        for d in range(2):
            matrix = fixed[d] - 0.5 * fock[d]
            fock[d] = matrix
            dens[d] = start[d] - damping * dot32(dot32(start[d], matrix), start[d])

    begin()

    def arriving(c, carry):
        load(c, 0).wait()
        load(c, 1).wait()

        @pl.when(c + 1 < CHUNKS)
        def _():
            load_chunk(c + 1)

        @pl.when(c == CHUNKS - 1)
        def _():
            for copy in late:
                copy.start()

        accumulate(c * per_chunk, per_chunk)
        return carry

    lax.fori_loop(0, CHUNKS, arriving, 0)
    for copy in late:
        copy.wait()
    fill_fixed()
    update()

    def sweep(t, carry):
        begin()

        def body(step, inner_carry):
            accumulate(step * STEP, STEP)
            return inner_carry

        lax.fori_loop(0, NAUX // STEP, body, 0)
        update()
        return carry

    lax.fori_loop(1, ITERS, sweep, 0)

    for d in range(2):
        matrix, density = fock[d], dens[d]
        energy[d] = (0.5 / NB2) * jnp.sum(density * (core_ham[d] + matrix))
        block = dot32(dot32(density, matrix), density)
        weighted[d] = jnp.where(left, block[:NB], block[NB:])
    for j in range(N_INNER):
        for d in range(2):
            blocks[j, d] = weighted[d, j * 8:(j + 1) * 8]


def route_kernel(pairs, got, out, count, owners, ranks):
    group = lax.axis_index("group")
    for o in range(N_GROUP):
        count[o] = 0
    for side in range(2):
        for dimer in range(DIM_GRP):
            owner = owner_of(pairs[side, group * DIM_GRP + dimer])
            rank = count[owner]
            owners[2 * dimer + side] = owner
            ranks[2 * dimer + side] = rank
            count[owner] = rank + 1
    out[...] = jnp.zeros_like(out)
    lane_half = iota((8, 128), 1) // NB
    for dimer in range(DIM_GRP):
        block = got[dimer // 2, dimer % 2]
        turned = pltpu.roll(block, NB, 1)
        for side in range(2):
            owner, rank = owners[2 * dimer + side], ranks[2 * dimer + side]
            half = lax.rem(rank, 2)
            value = jnp.where(half == side, block, turned)
            here = (owner, lax.div(rank, 2))
            out[here] = jnp.where(lane_half == half, value, out[here])


def home_kernel(table, got, out):
    out[...] = jnp.zeros_like(out)
    for g in range(N_GROUP):
        for s in range(CAP):
            at = table[s, g]
            block = got[g, s // 2]
            value = block[:, :NB] if s % 2 == 0 else pltpu.roll(block, NB, 1)[:, :NB]
            out[at] = out[at] + jnp.where(s < table[CAP, g], value, 0.0)


def params(mib):
    return pltpu.CompilerParams(vmem_limit_bytes=mib * 1024 * 1024)


def per_device(densities, ref_charge, site_pos, dimer_pairs, probe_pos, core_ham, probe_ints, ri_ints):
    f32, i32 = jnp.float32, jnp.int32
    pairs = dimer_pairs.T
    swap = [(i, i ^ 1) for i in range(N_INNER)]

    with jax.named_scope("pack"):
        send, table = pl.pallas_call(
            pack_kernel,
            out_shape=(jax.ShapeDtypeStruct((N_GROUP, ROWS, 128), f32),
                       jax.ShapeDtypeStruct((8, 128), i32)),
            in_specs=[VMEM, ANY, VMEM, VMEM],
            out_specs=(VMEM, VMEM),
            scratch_shapes=[pltpu.VMEM((FRAG_GRP, NB, NB), f32), pltpu.SMEM((8, 128), i32),
                            pltpu.SemaphoreType.DMA, pltpu.SemaphoreType.DMA],
            compiler_params=params(58),
            name="pack",
        )(pairs, densities, ref_charge.T, site_pos)
    mine = lax.all_to_all(send, "group", split_axis=0, concat_axis=0, tiled=True)
    other = lax.ppermute(mine, "inner", swap)

    with jax.named_scope("scf"):
        square = pltpu.VMEM((2, NB2, NB2), f32)
        blocks, energy = pl.pallas_call(
            scf_kernel,
            out_shape=(jax.ShapeDtypeStruct((N_INNER, 2, 8, 128), f32), jax.ShapeDtypeStruct((2,), f32)),
            in_specs=[SMEM, VMEM, SMEM, ANY, ANY, ANY, ANY, ANY],
            out_specs=(VMEM, SMEM),
            scratch_shapes=[
                pltpu.VMEM((2, NAUX, NB2, NB2), jnp.bfloat16),
                square, square, square,
                pltpu.VMEM((2, NB2, NB2), jnp.bfloat16),
                square,
                pltpu.VMEM((2, NB, NB2), f32),
                pltpu.VMEM((4, NB, 128), f32),
                pltpu.VMEM((2, N_GROUP, ROWS - NB, 128), f32),
                square,
                pltpu.VMEM((2, NPROBE, NB2, NB2), jnp.bfloat16),
                pltpu.SemaphoreType.DMA((CHUNKS, 2)),
                pltpu.SemaphoreType.DMA((4,)),
                pltpu.SemaphoreType.DMA((4,)),
            ],
            compiler_params=params(58),
            name="scf",
        )(pairs, pairs, probe_pos, mine, other, core_ham, probe_ints, ri_ints)
    rows = lax.all_to_all(blocks, "inner", split_axis=0, concat_axis=0, tiled=True)

    with jax.named_scope("route"):
        slots = pl.pallas_call(
            route_kernel,
            out_shape=jax.ShapeDtypeStruct((N_GROUP, CAP // 2, 8, 128), f32),
            in_specs=[SMEM, VMEM],
            out_specs=VMEM,
            scratch_shapes=[pltpu.SMEM((N_GROUP,), i32), pltpu.SMEM((2 * DIM_GRP,), i32),
                            pltpu.SMEM((2 * DIM_GRP,), i32)],
            name="route",
        )(pairs, rows)
    homed = lax.all_to_all(slots, "group", split_axis=0, concat_axis=0, tiled=True)

    with jax.named_scope("home"):
        frag_weight = pl.pallas_call(
            home_kernel,
            out_shape=jax.ShapeDtypeStruct((FRAG_GRP, 8, NB), f32),
            in_specs=[SMEM, VMEM],
            out_specs=VMEM,
            name="home",
        )(table, homed)
    return (frag_weight, energy)


def solution(mesh):
    in_specs = (
        P("group", None, None),
        P("group", None),
        P(None, "group"),
        P(),
        P(None, ("group", "inner")),
        P(("group", "inner"), None, None),
        P(("group", "inner"), None, None, None),
        P(("group", "inner"), None, None, None),
    )
    out_specs = (P("group", "inner", None), P(("group", "inner")))
    return jax.shard_map(
        per_device, mesh=mesh, in_specs=in_specs, out_specs=out_specs, check_vma=False
    )
```

time: 105 us -> 91 us (0.87)
  blocking collectives: 32.5 us -> 42.9 us
  local copies, waits for them, and re-layouts: 8.89 us -> 0.84 us
  Pallas kernels: 50.8 us -> 43.9 us
  starting transfers between devices: 6.03 us -> 0.01 us
  waiting for transfers between devices: 4.95 us -> 2.09 us
    all_to_all x0 -> x1, blocking collectives: none -> 10.2 us  [per_device(): lax.all_to_all(blocks, 'inner', split_axis=0, concat_axis=0, tiled=True)]
    unnamed x24 -> x4, local copies, waits for them, and re-layouts: 7.69 us -> 0.84 us
    ppermute x4 -> x0, starting transfers between devices: 6.03 us -> none  [the longest x3 5.82 us: per_device(): got.append(lax.ppermute(jnp.stack([keep[k], partner[k]]), 'inner', step))]
    pallas_call x1, Pallas kernels: 41.3 us -> 36.3 us  [per_device(): pl.pallas_call(scf_kernel, out_shape=(jax.ShapeDtypeStruct((N_INNER, 2, 8...]
    ppermute x4 -> x0, waiting for transfers between devices: 2.86 us -> none  [the longest x3 2.38 us: per_device(): got.append(lax.ppermute(jnp.stack([keep[k], partner[k]]), 'inner', step))]
    slice x2 -> x0, local copies, waits for them, and re-layouts: 1.2 us -> none  [per_device(): got.append(lax.ppermute(jnp.stack([keep[k], partner[k]]), 'inner', step))]
  transfers between devices with their start and end apart: 5 -> 1, of which waited for: 4 -> 1; matrix products, arithmetic and copies ran while one was open for 1% -> 0% of each run, Pallas kernels for 0% -> 0%
where the time goes in v1:
time: 91 us; the launch traced here: 90.4 us
  Pallas kernels  43.9 us (48%)
  blocking collectives  42.9 us (47%)
  waiting for transfers between devices  2.09 us (2%)
    pallas_call x1, Pallas kernels, per_device(): pl.pallas_call(scf_kernel, out_shape=(jax.ShapeDtypeStruct((N_INNER, 2, 8...  36.3 us
    all_to_all x1, blocking collectives, per_device(): lax.all_to_all(send, 'group', split_axis=0, concat_axis=0, tiled=True)  20.7 us
    all_to_all x1, blocking collectives, per_device(): lax.all_to_all(slots, 'group', split_axis=0, concat_axis=0, tiled=True)  12 us
    all_to_all x1, blocking collectives, per_device(): lax.all_to_all(blocks, 'inner', split_axis=0, concat_axis=0, tiled=True)  10.2 us
    pallas_call x1, Pallas kernels, per_device(): pl.pallas_call(pack_kernel, out_shape=(jax.ShapeDtypeStruct((N_GROUP, ROW...  3.87 us
    ppermute x1, waiting for transfers between devices, per_device(): other = lax.ppermute(mine, 'inner', swap)  2.09 us
    pallas_call x1, Pallas kernels, per_device(): pl.pallas_call(home_kernel, out_shape=jax.ShapeDtypeStruct((FRAG_GRP, 8,...  1.98 us
  transfers between devices with their start and end apart: 1, of which 1 were waited for; matrix products, arithmetic and copies ran while one was open for 0% of the time, Pallas kernels for 0%

profile of v1, /device:TPU:0, one launch (start us, length us, event | category | flops | bytes accessed | tf_op | source)
XLA Modules:
  0.0 90.4 jit_solution(16356219506907762759)
XLA Ops:
  0.6 3.9 %pack.1 = (f32[16,80,128]{2,1,0:T(8,128)}, s32[8,128]{1,0:T(8,128)}) custom-call(s32[2,256]{1,0:T(2,128)} %bitcast.2, f32[64,64,64]{2,1,0:T(8,128)} %dens_hbm.1, f32[16,64]{1,0:T(8,128)} %bitcast.6, f32[3,1024]{1,0:T(4,128)} %site_pos.1), custom_call_target="tpu_custom_call" | custom-call | tf_op jit(solution)/shard_map/pack/pack/pallas_call | solution.py:324
  4.5 20.7 %all_to_all.15.mine = f32[16,80,128]{2,1,0:T(8,128)S(1)} all-to-all(f32[16,80,128]{2,1,0:T(8,128)} %get-tuple-element.7), channel_id=1, replica_groups=mesh['group'=16,'inner'=8] {'group'}, dimensions={0} | all-to-all | bytes 1310720 | tf_op jit(solution)/shard_map/all_to_all | solution.py:335
  25.2 0.0 copy-start
  25.2 0.0 collective-permute-start
  25.2 2.1 %collective-permute-done.other = f32[16,80,128]{2,1,0:T(8,128)S(1)} collective-permute-done((f32[16,80,128]{2,1,0:T(8,128)S(1)}, f32[16,80,128]{2,1,0:T(8,128)S(1)}, u32[]{:S(2)}, u32[]{:S(2)}) %collective-permute-start) | collective-permute-done | bytes 655392 | tf_op jit(solution)/shard_map/ppermute | solution.py:336
  27.3 0.0 copy-done
  27.3 0.0 copy-start.1
  27.3 0.8 copy-done.1
  28.2 36.3 %scf.1 = (f32[8,2,8,128]{3,2,1,0:T(8,128)}, f32[2]{0:T(128)}) custom-call(s32[2,256]{1,0:T(2,128)} %bitcast.3, s32[2,256]{1,0:T(2,128)} %bitcast.4, f32[3,16]{1,0:T(4,128)} %probe_pos.1, f32[16,80,128]{2,1,0:T(8,128)} %copy-done, f32[16,80,128]{2,1,0:T(8,128)} %copy-done.1, f32[2,128,128]{2,1,0:T(8,128)} %core_any.1, bf16[2,8,128,128]{3,2,1,0:T(8,128)(2,1)} %probes_any.1, ...), custom_call_target="tpu_custom_call" | custom-call | tf_op jit(solution)/shard_map/scf/scf/pallas_call | solution.py:340
  64.5 10.2 %all_to_all.16.got = f32[8,2,8,128]{3,2,1,0:T(8,128)} all-to-all(f32[8,2,8,128]{3,2,1,0:T(8,128)} %get-tuple-element.8), channel_id=1, replica_groups=mesh['group'=16,'inner'=8] {'inner'}, dimensions={0} | all-to-all | bytes 131072 | tf_op jit(solution)/shard_map/all_to_all | solution.py:362
  74.7 1.8 %route.1 = f32[16,2,8,128]{3,2,1,0:T(8,128)} custom-call(s32[2,256]{1,0:T(2,128)} %bitcast.5, f32[8,2,8,128]{3,2,1,0:T(8,128)} %all_to_all.16.got), custom_call_target="tpu_custom_call" | custom-call | tf_op jit(solution)/shard_map/route/route/pallas_call | solution.py:365
  76.5 12.0 %all_to_all.17.got = f32[16,2,8,128]{3,2,1,0:T(8,128)} all-to-all(f32[16,2,8,128]{3,2,1,0:T(8,128)} %route.1), channel_id=1, replica_groups=mesh['group'=16,'inner'=8] {'group'}, dimensions={0} | all-to-all | bytes 262144 | tf_op jit(solution)/shard_map/all_to_all | solution.py:374
  88.4 2.0 %home.1 = f32[64,8,64]{2,1,0:T(8,128)} custom-call(s32[8,128]{1,0:T(8,128)} %get-tuple-element.6.table, f32[16,2,8,128]{3,2,1,0:T(8,128)} %all_to_all.17.got), custom_call_target="tpu_custom_call" | custom-call | tf_op jit(solution)/shard_map/home/home/pallas_call | solution.py:377
Async XLA Ops:
  25.2 2.1 %copy-start = (f32[16,80,128]{2,1,0:T(8,128)}, f32[16,80,128]{2,1,0:T(8,128)S(1)}, u32[]{:S(2)}) copy-start(f32[16,80,128]{2,1,0:T(8,128)S(1)} %all_to_all.15.mine) | copy-start | bytes 1966084
  25.2 2.1 %collective-permute-start = (f32[16,80,128]{2,1,0:T(8,128)S(1)}, f32[16,80,128]{2,1,0:T(8,128)S(1)}, u32[]{:S(2)}, u32[]{:S(2)}) collective-permute-start(f32[16,80,128]{2,1,0:T(8,128)S(1)} %all_to_all.15.mine), channel_id=1, source_target_pairs={{0,1},{1,0},{2,3},{3,2},{4,5},{5,4},{6,7},{7,6},{8,9},{9,8},{10,11... | collective-permute-start | bytes 1966088 | tf_op jit(solution)/shard_map/ppermute | solution.py:336
  27.3 0.8 copy-start.1

commit v2 on v1

--- a/solution.py
+++ b/solution.py
@@ -18,7 +18,8 @@
 N_INNER = 8
 SITE_ROWS = 8
 HALF = SITE_ROWS // 2
-ROWS = NB + 4 * HALF
+TRI = NB - NB // 4
+ROWS = TRI + 4 * HALF
 
 STEP = 128
 PART = 4
@@ -101,10 +102,12 @@
     sites = jnp.concatenate(sites + [jnp.where(core == 0, charge[:HALF], charge[HALF:])], axis=0)
 
     tell.wait()
+    inner_half = iota((NB // 4, 128), 1) % NB < NB // 2
     for g in range(N_GROUP):
-        pair = [dens[found[2 * core + s, g]] for s in range(2)]
-        send[g, :NB] = jnp.concatenate(pair, axis=1)
-        send[g, NB:] = sites
+        pair = jnp.concatenate([dens[found[2 * core + s, g]] for s in range(2)], axis=1)
+        send[g, :NB // 2] = pair[:NB // 2]
+        send[g, NB // 2:TRI] = jnp.where(inner_half, pltpu.roll(pair[TRI:], 128 - NB // 2, 1), pair[NB // 2:TRI])
+        send[g, TRI:] = sites
 
 
 def scf_kernel(pairs, pairs_wide, probe_pos, mine, other, core_any, probes_any, ri_hbm,
@@ -143,29 +146,33 @@
 
         @pl.when(rank // 2 == core)
         def _():
-            pltpu.make_async_copy(mine.at[owner, pl.ds(0, NB)], frags.at[i], frag_sems.at[i]).start()
+            pltpu.make_async_copy(mine.at[owner, pl.ds(0, TRI)], frags.at[i], frag_sems.at[i]).start()
 
         @pl.when(rank // 2 != core)
         def _():
-            pltpu.make_async_copy(other.at[owner, pl.ds(0, NB)], frags.at[i], frag_sems.at[i]).start()
+            pltpu.make_async_copy(other.at[owner, pl.ds(0, TRI)], frags.at[i], frag_sems.at[i]).start()
 
         return rank
 
     ranks = [load_fragment(i) for i in range(4)]
-    late = [pltpu.make_async_copy(mine.at[:, pl.ds(NB, ROWS - NB)], sites.at[0], late_sems.at[0]),
-            pltpu.make_async_copy(other.at[:, pl.ds(NB, ROWS - NB)], sites.at[1], late_sems.at[1]),
+    late = [pltpu.make_async_copy(mine.at[:, pl.ds(TRI, ROWS - TRI)], sites.at[0], late_sems.at[0]),
+            pltpu.make_async_copy(other.at[:, pl.ds(TRI, ROWS - TRI)], sites.at[1], late_sems.at[1]),
             pltpu.make_async_copy(core_any, core_ham, late_sems.at[2]),
             pltpu.make_async_copy(probes_any, probe_ints, late_sems.at[3])]
 
+    lane, line = iota((NB2, NB2), 1), iota((NB2, NB2), 0)
+    mirrored = jnp.logical_and(line // (NB // 2) == lane // (NB // 2) + 1, line // NB == lane // NB)
+    stored = jnp.logical_and(line // NB == lane // NB, jnp.logical_not(mirrored))
     for d in range(2):
-        halves = []
+        lines = []
         for side in range(2):
             i = 2 * d + side
-            pltpu.make_async_copy(mine.at[0, pl.ds(0, NB)], frags.at[i], frag_sems.at[i]).wait()
+            pltpu.make_async_copy(mine.at[0, pl.ds(0, TRI)], frags.at[i], frag_sems.at[i]).wait()
             rows = frags[i]
-            halves.append(jnp.where(ranks[i] % 2 == side, rows, pltpu.roll(rows, NB, 1)))
-        start[d, :NB] = jnp.where(left, halves[0], 0.0)
-        start[d, NB:] = jnp.where(left, 0.0, halves[1])
+            rows = jnp.where(ranks[i] % 2 == side, rows, pltpu.roll(rows, NB, 1))
+            lines += [rows, pltpu.roll(rows[NB // 2:], NB // 2, 1)]
+        upper = jnp.where(stored, jnp.concatenate(lines, axis=0), 0.0)
+        start[d] = jnp.where(mirrored, upper.T, upper)
         dens[d] = start[d]
 
     def fill_fixed():
@@ -348,8 +355,8 @@
                 pltpu.VMEM((2, NB2, NB2), jnp.bfloat16),
                 square,
                 pltpu.VMEM((2, NB, NB2), f32),
-                pltpu.VMEM((4, NB, 128), f32),
-                pltpu.VMEM((2, N_GROUP, ROWS - NB, 128), f32),
+                pltpu.VMEM((4, TRI, 128), f32),
+                pltpu.VMEM((2, N_GROUP, ROWS - TRI, 128), f32),
                 square,
                 pltpu.VMEM((2, NPROBE, NB2, NB2), jnp.bfloat16),
                 pltpu.SemaphoreType.DMA((CHUNKS, 2)),

time: 91 us -> 90.1 us (level)
  blocking collectives: 42.9 us -> 41.7 us
    all_to_all x1, blocking collectives: 20.7 us -> 19.5 us  [per_device(): lax.all_to_all(send, 'group', split_axis=0, concat_axis=0, tiled=True)]
where the time goes in v2:
time: 90.1 us; the launch traced here: 89.5 us
  Pallas kernels  44.5 us (49%)
  blocking collectives  41.7 us (46%)
  waiting for transfers between devices  1.91 us (2%)
    pallas_call x1, Pallas kernels, per_device(): pl.pallas_call(scf_kernel, out_shape=(jax.ShapeDtypeStruct((N_INNER, 2, 8...  36.7 us
    all_to_all x1, blocking collectives, per_device(): lax.all_to_all(send, 'group', split_axis=0, concat_axis=0, tiled=True)  19.5 us
    all_to_all x1, blocking collectives, per_device(): lax.all_to_all(slots, 'group', split_axis=0, concat_axis=0, tiled=True)  12 us
    all_to_all x1, blocking collectives, per_device(): lax.all_to_all(blocks, 'inner', split_axis=0, concat_axis=0, tiled=True)  10.2 us
    pallas_call x1, Pallas kernels, per_device(): pl.pallas_call(pack_kernel, out_shape=(jax.ShapeDtypeStruct((N_GROUP, ROW...  4.09 us
    pallas_call x1, Pallas kernels, per_device(): pl.pallas_call(home_kernel, out_shape=jax.ShapeDtypeStruct((FRAG_GRP, 8,...  1.95 us
    ppermute x1, waiting for transfers between devices, per_device(): other = lax.ppermute(mine, 'inner', swap)  1.91 us
  transfers between devices with their start and end apart: 1, of which 1 were waited for; matrix products, arithmetic and copies ran while one was open for 0% of the time, Pallas kernels for 0%

profile of v2, /device:TPU:0, one launch (start us, length us, event | category | flops | bytes accessed | tf_op | source)
XLA Modules:
  0.0 89.5 jit_solution(18071767289244914033)
XLA Ops:
  0.6 4.1 %pack.1 = (f32[16,64,128]{2,1,0:T(8,128)}, s32[8,128]{1,0:T(8,128)}) custom-call(s32[2,256]{1,0:T(2,128)} %bitcast.2, f32[64,64,64]{2,1,0:T(8,128)} %dens_hbm.1, f32[16,64]{1,0:T(8,128)} %bitcast.6, f32[3,1024]{1,0:T(4,128)} %site_pos.1), custom_call_target="tpu_custom_call" | custom-call | tf_op jit(solution)/shard_map/pack/pack/pallas_call | solution.py:331
  4.7 19.5 %all_to_all.15.mine = f32[16,64,128]{2,1,0:T(8,128)S(1)} all-to-all(f32[16,64,128]{2,1,0:T(8,128)} %get-tuple-element.7), channel_id=1, replica_groups=mesh['group'=16,'inner'=8] {'group'}, dimensions={0} | all-to-all | bytes 1048576 | tf_op jit(solution)/shard_map/all_to_all | solution.py:342
  24.2 0.0 copy-start
  24.2 0.0 collective-permute-start
  24.2 1.9 %collective-permute-done.other = f32[16,64,128]{2,1,0:T(8,128)S(1)} collective-permute-done((f32[16,64,128]{2,1,0:T(8,128)S(1)}, f32[16,64,128]{2,1,0:T(8,128)S(1)}, u32[]{:S(2)}, u32[]{:S(2)}) %collective-permute-start) | collective-permute-done | bytes 524320 | tf_op jit(solution)/shard_map/ppermute | solution.py:343
  26.1 0.0 copy-done
  26.1 0.0 copy-start.1
  26.1 0.8 copy-done.1
  26.9 36.7 %scf.1 = (f32[8,2,8,128]{3,2,1,0:T(8,128)}, f32[2]{0:T(128)}) custom-call(s32[2,256]{1,0:T(2,128)} %bitcast.3, s32[2,256]{1,0:T(2,128)} %bitcast.4, f32[3,16]{1,0:T(4,128)} %probe_pos.1, f32[16,64,128]{2,1,0:T(8,128)} %copy-done, f32[16,64,128]{2,1,0:T(8,128)} %copy-done.1, f32[2,128,128]{2,1,0:T(8,128)} %core_any.1, bf16[2,8,128,128]{3,2,1,0:T(8,128)(2,1)} %probes_any.1, ...), custom_call_target="tpu_custom_call" | custom-call | tf_op jit(solution)/shard_map/scf/scf/pallas_call | solution.py:347
  63.6 10.2 %all_to_all.16.got = f32[8,2,8,128]{3,2,1,0:T(8,128)} all-to-all(f32[8,2,8,128]{3,2,1,0:T(8,128)} %get-tuple-element.8), channel_id=1, replica_groups=mesh['group'=16,'inner'=8] {'inner'}, dimensions={0} | all-to-all | bytes 131072 | tf_op jit(solution)/shard_map/all_to_all | solution.py:369
  73.8 1.8 %route.1 = f32[16,2,8,128]{3,2,1,0:T(8,128)} custom-call(s32[2,256]{1,0:T(2,128)} %bitcast.5, f32[8,2,8,128]{3,2,1,0:T(8,128)} %all_to_all.16.got), custom_call_target="tpu_custom_call" | custom-call | tf_op jit(solution)/shard_map/route/route/pallas_call | solution.py:372
  75.6 12.0 %all_to_all.17.got = f32[16,2,8,128]{3,2,1,0:T(8,128)} all-to-all(f32[16,2,8,128]{3,2,1,0:T(8,128)} %route.1), channel_id=1, replica_groups=mesh['group'=16,'inner'=8] {'group'}, dimensions={0} | all-to-all | bytes 262144 | tf_op jit(solution)/shard_map/all_to_all | solution.py:381
  87.5 2.0 %home.1 = f32[64,8,64]{2,1,0:T(8,128)} custom-call(s32[8,128]{1,0:T(8,128)} %get-tuple-element.6.table, f32[16,2,8,128]{3,2,1,0:T(8,128)} %all_to_all.17.got), custom_call_target="tpu_custom_call" | custom-call | tf_op jit(solution)/shard_map/home/home/pallas_call | solution.py:384
Async XLA Ops:
  24.2 1.9 %copy-start = (f32[16,64,128]{2,1,0:T(8,128)}, f32[16,64,128]{2,1,0:T(8,128)S(1)}, u32[]{:S(2)}) copy-start(f32[16,64,128]{2,1,0:T(8,128)S(1)} %all_to_all.15.mine) | copy-start | bytes 1572868
  24.2 1.9 %collective-permute-start = (f32[16,64,128]{2,1,0:T(8,128)S(1)}, f32[16,64,128]{2,1,0:T(8,128)S(1)}, u32[]{:S(2)}, u32[]{:S(2)}) collective-permute-start(f32[16,64,128]{2,1,0:T(8,128)S(1)} %all_to_all.15.mine), channel_id=1, source_target_pairs={{0,1},{1,0},{2,3},{3,2},{4,5},{5,4},{6,7},{7,6},{8,9},{9,8},{10,11... | collective-permute-start | bytes 1572872 | tf_op jit(solution)/shard_map/ppermute | solution.py:343
  26.1 0.8 copy-start.1

commit v3 on v2

--- a/solution.py
+++ b/solution.py
@@ -18,7 +18,7 @@
 N_INNER = 8
 SITE_ROWS = 8
 HALF = SITE_ROWS // 2
-TRI = NB - NB // 4
+TRI = NB // 2 + 8
 ROWS = TRI + 4 * HALF
 
 STEP = 128
@@ -102,11 +102,14 @@
     sites = jnp.concatenate(sites + [jnp.where(core == 0, charge[:HALF], charge[HALF:])], axis=0)
 
     tell.wait()
-    inner_half = iota((NB // 4, 128), 1) % NB < NB // 2
+    line, lane = iota((NB // 2, 128), 0), iota((NB // 2, 128), 1) % NB
+    spare = line > lane
+    on_diagonal = line == lane - NB // 2
     for g in range(N_GROUP):
         pair = jnp.concatenate([dens[found[2 * core + s, g]] for s in range(2)], axis=1)
-        send[g, :NB // 2] = pair[:NB // 2]
-        send[g, NB // 2:TRI] = jnp.where(inner_half, pltpu.roll(pair[TRI:], 128 - NB // 2, 1), pair[NB // 2:TRI])
+        lower = pair[NB // 2:]
+        send[g, :NB // 2] = jnp.where(spare, pltpu.roll(lower, 128 - NB // 2, 1), pair[:NB // 2])
+        send[g, NB // 2:TRI] = jnp.sum(jnp.where(on_diagonal, lower, 0.0).reshape(-1, 8, 128), axis=0)
         send[g, TRI:] = sites
 
 
@@ -161,8 +164,11 @@
             pltpu.make_async_copy(probes_any, probe_ints, late_sems.at[3])]
 
     lane, line = iota((NB2, NB2), 1), iota((NB2, NB2), 0)
-    mirrored = jnp.logical_and(line // (NB // 2) == lane // (NB // 2) + 1, line // NB == lane // NB)
-    stored = jnp.logical_and(line // NB == lane // NB, jnp.logical_not(mirrored))
+    same = line // NB == lane // NB
+    top, left_half = line % NB < NB // 2, lane % NB < NB // 2
+    stored = jnp.logical_or(jnp.logical_and(top, jnp.logical_or(line <= lane, jnp.logical_not(left_half))),
+                            jnp.logical_and(jnp.logical_not(left_half), line >= lane))
+    low_diagonal = iota((NB // 2, NB2), 0) + NB // 2 == iota((NB // 2, NB2), 1) % NB
     for d in range(2):
         lines = []
         for side in range(2):
@@ -170,9 +176,11 @@
             pltpu.make_async_copy(mine.at[0, pl.ds(0, TRI)], frags.at[i], frag_sems.at[i]).wait()
             rows = frags[i]
             rows = jnp.where(ranks[i] % 2 == side, rows, pltpu.roll(rows, NB, 1))
-            lines += [rows, pltpu.roll(rows[NB // 2:], NB // 2, 1)]
-        upper = jnp.where(stored, jnp.concatenate(lines, axis=0), 0.0)
-        start[d] = jnp.where(mirrored, upper.T, upper)
+            upper = rows[:NB // 2]
+            low = jnp.concatenate([rows[NB // 2:]] * (NB // 16), axis=0)
+            lines += [upper, jnp.where(low_diagonal, low, pltpu.roll(upper, NB // 2, 1))]
+        packed_once = jnp.concatenate(lines, axis=0)
+        start[d] = jnp.where(same, jnp.where(stored, packed_once, packed_once.T), 0.0)
         dens[d] = start[d]
 
     def fill_fixed():

time: 90.1 us -> 89.4 us (level)
  no operation moved by 1% of the time
where the time goes in v3:
time: 89.4 us; the launch traced here: 88.8 us
  Pallas kernels  44.6 us (50%)
  blocking collectives  41 us (46%)
  waiting for transfers between devices  1.81 us (2%)
    pallas_call x1, Pallas kernels, per_device(): pl.pallas_call(scf_kernel, out_shape=(jax.ShapeDtypeStruct((N_INNER, 2, 8...  36.7 us
    all_to_all x1, blocking collectives, per_device(): lax.all_to_all(send, 'group', split_axis=0, concat_axis=0, tiled=True)  18.8 us
    all_to_all x1, blocking collectives, per_device(): lax.all_to_all(slots, 'group', split_axis=0, concat_axis=0, tiled=True)  12 us
    all_to_all x1, blocking collectives, per_device(): lax.all_to_all(blocks, 'inner', split_axis=0, concat_axis=0, tiled=True)  10.2 us
    pallas_call x1, Pallas kernels, per_device(): pl.pallas_call(pack_kernel, out_shape=(jax.ShapeDtypeStruct((N_GROUP, ROW...  4.2 us
    pallas_call x1, Pallas kernels, per_device(): pl.pallas_call(home_kernel, out_shape=jax.ShapeDtypeStruct((FRAG_GRP, 8,...  1.97 us
    ppermute x1, waiting for transfers between devices, per_device(): other = lax.ppermute(mine, 'inner', swap)  1.81 us
  transfers between devices with their start and end apart: 1, of which 1 were waited for; matrix products, arithmetic and copies ran while one was open for 0% of the time, Pallas kernels for 0%

profile of v3, /device:TPU:0, one launch (start us, length us, event | category | flops | bytes accessed | tf_op | source)
XLA Modules:
  0.0 88.8 jit_solution(1792559795693497698)
XLA Ops:
  0.6 4.2 %pack.1 = (f32[16,56,128]{2,1,0:T(8,128)}, s32[8,128]{1,0:T(8,128)}) custom-call(s32[2,256]{1,0:T(2,128)} %bitcast.2, f32[64,64,64]{2,1,0:T(8,128)} %dens_hbm.1, f32[16,64]{1,0:T(8,128)} %bitcast.6, f32[3,1024]{1,0:T(4,128)} %site_pos.1), custom_call_target="tpu_custom_call" | custom-call | tf_op jit(solution)/shard_map/pack/pack/pallas_call | solution.py:339
  4.8 18.8 %all_to_all.15.mine = f32[16,56,128]{2,1,0:T(8,128)S(1)} all-to-all(f32[16,56,128]{2,1,0:T(8,128)} %get-tuple-element.7), channel_id=1, replica_groups=mesh['group'=16,'inner'=8] {'group'}, dimensions={0} | all-to-all | bytes 917504 | tf_op jit(solution)/shard_map/all_to_all | solution.py:350
  23.6 0.0 copy-start
  23.6 0.0 collective-permute-start
  23.6 1.8 %collective-permute-done.other = f32[16,56,128]{2,1,0:T(8,128)S(1)} collective-permute-done((f32[16,56,128]{2,1,0:T(8,128)S(1)}, f32[16,56,128]{2,1,0:T(8,128)S(1)}, u32[]{:S(2)}, u32[]{:S(2)}) %collective-permute-start) | collective-permute-done | bytes 458784 | tf_op jit(solution)/shard_map/ppermute | solution.py:351
  25.4 0.0 copy-done
  25.4 0.0 copy-start.1
  25.4 0.8 copy-done.1
  26.2 36.7 %scf.1 = (f32[8,2,8,128]{3,2,1,0:T(8,128)}, f32[2]{0:T(128)}) custom-call(s32[2,256]{1,0:T(2,128)} %bitcast.3, s32[2,256]{1,0:T(2,128)} %bitcast.4, f32[3,16]{1,0:T(4,128)} %probe_pos.1, f32[16,56,128]{2,1,0:T(8,128)} %copy-done, f32[16,56,128]{2,1,0:T(8,128)} %copy-done.1, f32[2,128,128]{2,1,0:T(8,128)} %core_any.1, bf16[2,8,128,128]{3,2,1,0:T(8,128)(2,1)} %probes_any.1, ...), custom_call_target="tpu_custom_call" | custom-call | tf_op jit(solution)/shard_map/scf/scf/pallas_call | solution.py:355
  62.9 10.2 %all_to_all.16.got = f32[8,2,8,128]{3,2,1,0:T(8,128)} all-to-all(f32[8,2,8,128]{3,2,1,0:T(8,128)} %get-tuple-element.8), channel_id=1, replica_groups=mesh['group'=16,'inner'=8] {'inner'}, dimensions={0} | all-to-all | bytes 131072 | tf_op jit(solution)/shard_map/all_to_all | solution.py:377
  73.1 1.8 %route.1 = f32[16,2,8,128]{3,2,1,0:T(8,128)} custom-call(s32[2,256]{1,0:T(2,128)} %bitcast.5, f32[8,2,8,128]{3,2,1,0:T(8,128)} %all_to_all.16.got), custom_call_target="tpu_custom_call" | custom-call | tf_op jit(solution)/shard_map/route/route/pallas_call | solution.py:380
  74.9 12.0 %all_to_all.17.got = f32[16,2,8,128]{3,2,1,0:T(8,128)} all-to-all(f32[16,2,8,128]{3,2,1,0:T(8,128)} %route.1), channel_id=1, replica_groups=mesh['group'=16,'inner'=8] {'group'}, dimensions={0} | all-to-all | bytes 262144 | tf_op jit(solution)/shard_map/all_to_all | solution.py:389
  86.9 2.0 %home.1 = f32[64,8,64]{2,1,0:T(8,128)} custom-call(s32[8,128]{1,0:T(8,128)} %get-tuple-element.6.table, f32[16,2,8,128]{3,2,1,0:T(8,128)} %all_to_all.17.got), custom_call_target="tpu_custom_call" | custom-call | tf_op jit(solution)/shard_map/home/home/pallas_call | solution.py:392
Async XLA Ops:
  23.6 1.8 %copy-start = (f32[16,56,128]{2,1,0:T(8,128)}, f32[16,56,128]{2,1,0:T(8,128)S(1)}, u32[]{:S(2)}) copy-start(f32[16,56,128]{2,1,0:T(8,128)S(1)} %all_to_all.15.mine) | copy-start | bytes 1376260
  23.6 1.8 %collective-permute-start = (f32[16,56,128]{2,1,0:T(8,128)S(1)}, f32[16,56,128]{2,1,0:T(8,128)S(1)}, u32[]{:S(2)}, u32[]{:S(2)}) collective-permute-start(f32[16,56,128]{2,1,0:T(8,128)S(1)} %all_to_all.15.mine), channel_id=1, source_target_pairs={{0,1},{1,0},{2,3},{3,2},{4,5},{5,4},{6,7},{7,6},{8,9},{9,8},{10,11... | collective-permute-start | bytes 1376264 | tf_op jit(solution)/shard_map/ppermute | solution.py:351
  25.4 0.8 copy-start.1
